TPU v7x, 128 devices: a whole 4x4x4 slice. The times are simulated.
128 devices in a mesh: rows: 128 (over x, z, y, core).
Axes of the slice: x: 4, y: 4, z: 4, core: 2. Of those that a mesh axis runs over, the one named last changes fastest.
Arguments:
- seeds: int32 [512], P('rows'), may hold values from 0 to 16777215
- offset: int32 [1], replicated, may hold values from 0 to 64512
Outputs:
- field_real: float32 [32768, 1024], P('rows')
- field_imag: float32 [32768, 1024], P('rows')
All inputs are finite; a program needn't handle non-finite values.
Results may differ from a plain program's by a relative error of at most 0.00013.
Values sent between devices are 32-bit elements; how exact they have to be, the bound alone decides.
A program may use at most 64 MiB of HBM per device.

v0:
```python
import math

import jax
import jax.numpy as jnp
from jax import lax
from jax.sharding import PartitionSpec as P

NY = 32768
NXG = 65536
STRIP = 1024
KAPPA = 8192
SEED_BLOCK = 64


def uniform_noise(seed_grid, wave_grid, column_grid, salt):
    h = (seed_grid % 65521 + wave_grid * 7919 % 65521 + column_grid * 30011 % 65521 + salt) % 65521
    h = (h % 46337 * (h % 46337) + column_grid % 4099 * 7 + salt) % 65521
    h = (h * 32719 + wave_grid % 8191 * 13) % 65521
    h = (h % 46337 * (h % 46337) + seed_grid % 32749) % 65521
    unit = (h.astype(jnp.float32) + 0.5) / 65521.0
    return 3.4641016151377544 * (unit - 0.5)


def spectrum(seed_rows, waves, column):
    wave_x = jnp.minimum(column, NXG - column).astype(jnp.float32)
    wave_y = jnp.minimum(waves, NY - waves).astype(jnp.float32)
    radius = (wave_x[None, :] * wave_x[None, :] + wave_y[:, None] * wave_y[:, None]) / (
        float(KAPPA) * float(KAPPA)
    )
    amplitude = 2.0 * (1.0 + radius) ** (-0.75)
    seed_grid = seed_rows[:, None]
    wave_grid = waves[:, None]
    column_grid = column[None, :]
    noise_real = uniform_noise(seed_grid, wave_grid, column_grid, 17)
    noise_imag = uniform_noise(seed_grid, wave_grid, column_grid, 29011)
    return (amplitude * noise_real, amplitude * noise_imag)


def bit_reverse(index, levels):
    result = index * 0
    for level in range(levels):
        result = result + index // 2**level % 2 * 2 ** (levels - 1 - level)
    return result


def rotation_matrix(angle):
    cosine = jnp.cos(angle)
    sine = jnp.sin(angle)
    top = jnp.concatenate([cosine, -sine], axis=1)
    bottom = jnp.concatenate([sine, cosine], axis=1)
    return jnp.concatenate([top, bottom], axis=0)


def shards(seeds, offset):
    parts = lax.axis_size("rows")
    levels = parts.bit_length() - 1
    index = lax.axis_index("rows")
    depth = NY // parts
    all_seeds = lax.all_gather(seeds, "rows", axis=0, tiled=True)
    own = bit_reverse(index, levels)
    local = lax.iota(jnp.int32, depth)
    waves = own + parts * local
    blocks = lax.iota(jnp.int32, all_seeds.shape[0])
    match = (waves // SEED_BLOCK)[:, None] == blocks[None, :]
    seed_rows = jnp.sum(jnp.where(match, all_seeds[None, :], 0), axis=1)
    column = offset[0] + lax.iota(jnp.int32, STRIP)
    real_part, imag_part = spectrum(seed_rows, waves, column)
    stacked = jnp.concatenate([real_part, imag_part], axis=0)
    phase_steps = local[:, None] * local[None, :] % depth
    inner = rotation_matrix(phase_steps.astype(jnp.float32) * (2.0 * math.pi / depth))
    partial_sum = jnp.dot(
        inner, stacked, preferred_element_type=jnp.float32, precision=lax.Precision.HIGHEST
    )
    partial_sum = partial_sum.reshape(2, depth, STRIP)
    twist = (own * local % NY).astype(jnp.float32) * (2.0 * math.pi / NY)
    twist_cos = jnp.cos(twist)[:, None]
    twist_sin = jnp.sin(twist)[:, None]
    turned_real = twist_cos * partial_sum[0] - twist_sin * partial_sum[1]
    turned_imag = twist_sin * partial_sum[0] + twist_cos * partial_sum[1]
    turned = jnp.stack([turned_real, turned_imag])
    share = depth // parts
    sources = lax.iota(jnp.int32, parts)
    outer_steps = sources[:, None] * bit_reverse(sources, levels)[None, :] % parts
    outer = rotation_matrix(outer_steps.astype(jnp.float32) * (2.0 * math.pi / parts))
    block = lax.all_to_all(turned, "rows", split_axis=1, concat_axis=1, tiled=True)
    count = block.shape[2]
    flat = block.reshape(2 * parts, share * count)
    mixed = jnp.dot(
        outer, flat, preferred_element_type=jnp.float32, precision=lax.Precision.HIGHEST
    )
    combined = mixed.reshape(2, parts * share, count)
    result = lax.all_to_all(combined, "rows", split_axis=1, concat_axis=1, tiled=True)
    result = result * NY ** (-0.5)
    return (result[0], result[1])


def solution(mesh):
    in_specs = (P("rows"), P())
    out_specs = (P("rows", None), P("rows", None))
    return jax.shard_map(shards, mesh=mesh, in_specs=in_specs, out_specs=out_specs, check_vma=False)
```

profile of v0, /device:TPU:1, one launch (start us, length us, event | category | flops | bytes accessed | tf_op | source)
XLA Modules:
  0.0 174.1 jit_solution(11664851044114439440)
XLA Ops:
  0.8 0.1 fusion.99
  0.9 1.0 fusion.75
  1.9 1.0 fusion.77
  2.9 0.1 fusion.124
  2.9 0.9 dynamic-update-slice
  3.8 68.7 %all-reduce = s32[512]{0:T(512)S(1)} all-reduce(s32[512]{0:T(512)S(1)} %dynamic-update-slice), channel_id=1, replica_groups=mesh['rows'=128] {'rows'}, use_global_device_ids=true, to_apply=%add | all-reduce | flops 512 | bytes 4096
  72.5 0.2 select_reduce_fusion
  73.4 8.2 %fusion.29 = (f32[256,1024]{1,0:T(8,128)S(1)}, f32[256,1024]{1,0:T(8,128)S(1)}) fusion(s32[256]{0:T(256)S(1)} %get-tuple-element.9, s32[256]{0:T(256)S(1)} %get-tuple-element.13, s32[1024]{0:T(1024)S(1)} %get-tuple-element.17, s32[1024]{0:T(1024)S(1)} %get-tuple-element.16, s32[256]{0:T(256)S(1)} %get-tuple-element.8, f32[256]{0:T(256)S(1)} %get-tuple-element.14, ...), kind=kLoop, calls=%fused_computation.44 | loop fusion | flops 27525120 | bytes 2113536 | tf_op jit(solution)/shard_map/mul | solution.py:36
  81.6 3.6 %fusion = f32[512,1024]{1,0:T(8,128)S(1)} fusion(f32[256,1024]{1,0:T(8,128)S(1)} %get-tuple-element.7, f32[256,1024]{1,0:T(8,128)S(1)} %get-tuple-element.6, f32[256,256]{1,0:T(8,128)S(1)} %get-tuple-element.19, f32[256,256]{1,0:T(8,128)S(1)} %get-tuple-element.18, f32[256,256]{1,0:T(8,128)S(1)} %fusion.77), kind=kOutput, calls=%fused_computation | convolution fusion | flops 3222536192 | bytes 4980736 | tf_op jit(solution)/shard_map/dot_general | solution.py:71
  85.2 0.5 subtract_bitcast_fusion
  85.7 0.2 pad_maximum_fusion
  85.9 2.9 %copy.9 = f32[2,256,1024]{2,0,1:T(2,128)} copy(f32[2,256,1024]{2,1,0:T(8,128)S(1)} %pad_maximum_fusion) | data formatting | bytes 4194304 | tf_op jit(solution)/shard_map/stack | solution.py:80
  88.8 4.8 %all-to-all-start = ((f32[2,256,1024]{2,0,1:T(2,128)}), f32[2,256,1024]{2,0,1:T(2,128)S(1)}, u32[]{:S(2)}, u32[]{:S(2)}) async-start(f32[2,256,1024]{2,0,1:T(2,128)} %copy.9), calls=%async_computation | async-start | bytes 4194304 | tf_op jit(solution)/shard_map/all_to_all | solution.py:85
  93.6 0.3 fusion.86
  93.9 30.1 %all-to-all-done = f32[2,256,1024]{2,0,1:T(2,128)S(1)} async-done(((f32[2,256,1024]{2,0,1:T(2,128)}), f32[2,256,1024]{2,0,1:T(2,128)S(1)}, u32[]{:S(2)}, u32[]{:S(2)}) %all-to-all-start) | async-done | bytes 2097184 | tf_op jit(solution)/shard_map/all_to_all | solution.py:85
  124.0 2.0 %copy.10 = f32[2,256,1024]{2,1,0:T(8,128)} copy(f32[2,256,1024]{2,0,1:T(2,128)S(1)} %all-to-all-done) | data formatting | bytes 4194304 | tf_op jit(solution)/shard_map/all_to_all | solution.py:85
  126.0 1.9 %reshape.305 = f32[256,2048]{1,0:T(8,128)S(1)} reshape(f32[2,256,1024]{2,1,0:T(8,128)} %copy.10) | data formatting | bytes 4194304 | tf_op jit(solution)/shard_map/reshape | solution.py:87
  127.9 3.2 %fusion.64 = f32[256,2048]{1,0:T(8,128)} fusion(f32[256,2048]{1,0:T(8,128)S(1)} %reshape.305, f32[128,128]{1,0:T(8,128)S(1)} %get-tuple-element.12, f32[128,128]{1,0:T(8,128)S(1)} %get-tuple-element.11, f32[128,128]{1,0:T(8,128)S(1)} %get-tuple-element.10), kind=kOutput, calls=%fused_computation.90 | convolution fusion | flops 1610809344 | bytes 4390912 | tf_op jit(solution)/shard_map/dot_general | solution.py:88
  131.1 1.7 reshape.306
  132.8 1.6 copy.11
  134.5 34.6 %all_to_all.10 = f32[2,256,1024]{2,0,1:T(2,128)S(1)} all-to-all(f32[2,256,1024]{2,0,1:T(2,128)S(1)} %copy.11), channel_id=1, replica_groups=mesh['rows'=128] {'rows'}, dimensions={1} | all-to-all | bytes 4194304 | tf_op jit(solution)/shard_map/all_to_all | solution.py:92
  169.1 1.1 broadcast_multiply_fusion
  170.1 1.6 fusion.127
  171.8 1.2 copy.16
  172.9 1.2 copy.17
  (6 shorter events, 0.1 us)
Async XLA Ops:
  88.8 35.2 %all-to-all-start = ((f32[2,256,1024]{2,0,1:T(2,128)}), f32[2,256,1024]{2,0,1:T(2,128)S(1)}, u32[]{:S(2)}, u32[]{:S(2)}) async-start(f32[2,256,1024]{2,0,1:T(2,128)} %copy.9), calls=%async_computation | async-start | bytes 4194304 | tf_op jit(solution)/shard_map/all_to_all | solution.py:85
where the time goes:
time: 175 us; the launch traced here: 174 us
  blocking collectives  103 us (59%)
  waiting for transfers between devices  30.1 us (17%)
  local copies, waits for them, and re-layouts  15 us (9%)
  other arithmetic  12.7 us (7%)
  matrix products  6.79 us (4%)
  starting transfers between devices  4.76 us (3%)
    unnamed x1, blocking collectives  68.7 us
    all_to_all x1, blocking collectives, shards(): lax.all_to_all(combined, 'rows', split_axis=1, concat_axis=1, tiled=True)  34.6 us
    all_to_all x1, waiting for transfers between devices, shards(): lax.all_to_all(turned, 'rows', split_axis=1, concat_axis=1, tiled=True)  30.1 us
    mul x1, other arithmetic, spectrum(): return (amplitude * noise_real, amplitude * noise_imag)  8.19 us
    all_to_all x1, starting transfers between devices, shards(): lax.all_to_all(turned, 'rows', split_axis=1, concat_axis=1, tiled=True)  4.76 us
    dot_general x1, matrix products, shards(): jnp.dot(inner, stacked, preferred_element_type=jnp.float32, precision=lax...  3.58 us
  transfers between devices with their start and end apart: 1, of which 1 were waited for; matrix products, arithmetic and copies ran while one was open for 0% of the time, Pallas kernels for 0%

commit v1 on v0

v1 whole, which is shorter than its diff:
```python
import itertools
import math
import random

import jax
import jax.numpy as jnp
import ml_dtypes
import numpy as np
from jax import lax
from jax.experimental import pallas as pl
from jax.experimental.pallas import tpu as pltpu
from jax.sharding import PartitionSpec as P

NY = 32768
NXG = 65536
STRIP = 1024
KAPPA = 8192
N = 128
DEPTH = 256
PAIRS = 64
COLS = STRIP // PAIRS
NC = 4
CHUNKS = COLS // NC
Q = 2 * COLS
MOD = 65521
MESH = pl.DeviceIdType.MESH
F32 = jnp.float32
BF16 = jnp.bfloat16


def hops(offset):
    return sum((0, 1, 2, 1)[a] for a in offset[:3])


def is_near(offset):
    if hops(offset) != 3:
        return hops(offset) < 3
    if 2 not in offset[:3]:
        return sum(a == 3 for a in offset[:3]) % 2 == 0
    return (offset.index(0) + 1) % 3 == offset[:3].index(2)


def near_offsets():
    every = itertools.product(range(4), range(4), range(4), range(2))
    near = [offset for offset in every if is_near(offset)]
    random.Random(3).shuffle(near)
    return near


NEAR = near_offsets()


def tables():
    k1 = np.arange(N)[:, None]
    k2 = np.arange(DEPTH)[None, :]
    k = k1 + N * k2
    wave_hash = ((7919 * k) % MOD).astype(np.int32)
    wave_add = (13 * (k % 8191) + 16000 * MOD).astype(np.int32)
    ky = np.minimum(k, NY - k) / KAPPA
    wave_sq = (1.0 + ky * ky).astype(np.float32)
    angle = 2.0 * np.pi * (k1 * k2) / NY
    twist = np.stack([np.cos(angle), np.sin(angle)]).astype(np.float32)
    i = np.arange(DEPTH)
    angle = 2.0 * np.pi * (i[:, None] * i[None, :] % DEPTH) / DEPTH
    c, s = np.cos(angle), np.sin(angle)
    inner = np.block([[c, s], [-s, c]]).astype(np.float32)
    inner_hi = inner.astype(ml_dtypes.bfloat16)
    inner_lo = (inner - inner_hi.astype(np.float32)).astype(ml_dtypes.bfloat16)
    masks = [((a * 4 + b) * 4 + c) * 2 + d for a, b, c, d in NEAR]
    masks = np.broadcast_to(np.array(masks, np.int32)[:, None], (PAIRS, N))
    return (
        np.stack([wave_hash, wave_add]),
        wave_sq,
        twist,
        np.stack([inner_hi, inner_lo]),
        np.ascontiguousarray(masks),
    )


def split(x):
    hi = x.astype(BF16)
    return hi, (x - hi.astype(F32)).astype(BF16)


def mod_small(s, m):
    q = (s.astype(F32) * np.float32(1.0 / m)).astype(jnp.int32)
    r = s - q * m
    r = jnp.where(r < 0, r + m, r)
    return jnp.where(r >= m, r - m, r)


def noise(base, c1, c2, wave_add, seed_add):
    inv = np.float32(1.0 / MOD)
    t = base + c1
    t = jnp.where(t >= MOD, t - MOD, t)
    u = jnp.where(t >= 46337, t - 46337, t)
    p = u * u
    w = (p >> 16) * 32138 - (p & 0xFFFF) * 32802 + (wave_add + c2)
    w = w - (w >> 16) * MOD
    f = w.astype(F32)
    h = f - jnp.floor(f * inv + np.float32(0.5) * inv) * np.float32(MOD)
    u = jnp.where(h >= 46337.0, h - 46337.0, h).astype(jnp.int32)
    p = u * u + seed_add
    v = p - (p >> 16) * MOD
    x = v.astype(F32) * inv + np.float32(0.5 / MOD - 0.5)
    return x - jnp.round(x)


def xor_values(a):
    return [a, a + 1 - 2 * (a % 2), (a + 2) % 4, 3 - a]


def synth(
    offset, seeds, ints_hbm, wave_sq_hbm, twist_hbm, inner_hbm, masks_hbm, out,
    ints, seed2, wave_sq, twist, inner, masks, amp, xhi, xlo, ybuf, zbuf, outer,
    seed_row, seed_all, seeds_out, par, parf, tsem, gsem, grecv, ssem, rsem,
):
    me = lax.axis_index("rows")
    mx, mz, my, mc = me // 32, me // 8 % 4, me // 2 % 4, me % 2
    barrier = pltpu.get_barrier_semaphore()

    def greet(i, _):
        pl.semaphore_signal(barrier, inc=1, device_id=(lax.rem(me + i, N),), device_id_type=MESH)
        return 0

    lax.fori_loop(1, N, greet, 0)

    loads = [
        pltpu.make_async_copy(a, b, tsem.at[i])
        for i, (a, b) in enumerate(
            [(wave_sq_hbm, wave_sq), (masks_hbm, masks), (ints_hbm, ints), (inner_hbm, inner), (twist_hbm, twist)]
        )
    ]
    for load in loads:
        load.start()

    upper = mx // 2
    flip = lambda a: (a + 2 * upper) % 4
    pair = (mx % 2) * 32 + flip(mz) * 8 + flip(my) * 2 + mc

    lane = lax.broadcasted_iota(jnp.int32, (8, N), 1)
    odd, half = lane % 2, lane // 2 % 2
    seed_row[...] = jnp.where(
        half == 0, jnp.where(odd == 0, seeds[0], seeds[2]), jnp.where(odd == 0, seeds[1], seeds[3])
    )

    for j in range(COLS):
        g = offset[0] + (j * PAIRS + pair)
        c = g * 30011 % MOD
        d = g % 4099 * 7
        par[j, 0] = (c + 17) % MOD
        par[j, 1] = (c + 29011) % MOD
        par[j, 2] = (d + 17) * 32719 % MOD
        par[j, 3] = (d + 29011) * 32719 % MOD
        kx = jnp.minimum(g, NXG - g).astype(F32) * np.float32(1.0 / KAPPA)
        parf[j] = kx * kx

    loads[0].wait()
    loads[1].wait()
    dest = lax.bitwise_xor(masks[...], me)
    k1 = lax.broadcasted_iota(jnp.int32, (PAIRS, N), 1)
    angle = (dest * k1 % N).astype(F32) * np.float32(2.0 * math.pi / N)
    c, s = jnp.cos(angle), jnp.sin(angle)
    for x, i, k in ((c, 0, 0), (-s, 0, 1), (s, 1, 0), (c, 1, 1)):
        hi, lo = split(x)
        rows, cols = pl.ds(PAIRS * i, PAIRS), pl.ds(N * k, N)
        outer[0, rows, cols] = hi
        outer[1, rows, cols] = lo

    scale = np.float32(2.0 * 3.4641016151377544 / math.sqrt(NY))

    def amplitude(i, _):
        rows = pl.ds(pl.multiple_of(i * 16, 16), 16)
        z0 = wave_sq[rows]
        for j in range(COLS):
            y = lax.rsqrt(z0 + parf[j])
            amp[j, rows] = y * y * lax.rsqrt(y) * scale
        return 0

    lax.fori_loop(0, N // 16, amplitude, 0)

    for load in loads[2:]:
        load.wait()

    pl.semaphore_wait(barrier, N - 1)

    pltpu.make_async_copy(seed_row.at[0], seed_all.at[me], grecv).start()

    def seed_copy(i):
        return pltpu.make_async_remote_copy(
            src_ref=seed_row.at[0],
            dst_ref=seed_all.at[me],
            send_sem=gsem,
            recv_sem=grecv,
            device_id=(lax.rem(me + i, N),),
            device_id_type=MESH,
        )

    def send_seeds(i, _):
        seed_copy(i).start()
        return 0

    lax.fori_loop(1, N, send_seeds, 0)
    pltpu.make_async_copy(seed_all, seed_all, grecv).wait()

    got = seed_all[...]
    turned = pltpu.roll(got, 2, 1)
    lane = lax.broadcasted_iota(jnp.int32, (N, N), 1)
    row = lax.broadcasted_iota(jnp.int32, (N, N), 0)
    mine = lane // 2 == row % 64
    for h in range(2):
        picked = jnp.where(mine, jnp.where(lane // 2 % 2 == h, got, turned), 0).astype(F32)
        for t in range(2):
            s = jnp.sum(picked[64 * t : 64 * t + 64], axis=0, keepdims=True).astype(jnp.int32)
            rows, cols = pl.ds(64 * h, 64), pl.ds(128 * t, 128)
            a = ints[0, rows, cols] + jnp.broadcast_to(mod_small(s, MOD), (64, 128))
            ints[0, rows, cols] = jnp.where(a >= MOD, a - MOD, a)
            seed2[rows, cols] = jnp.broadcast_to(mod_small(s, 32749), (64, 128))

    xs, zs = [v * 32 for v in xor_values(mx)], [v * 8 for v in xor_values(mz)]
    ys, cs = [v * 2 for v in xor_values(my)], [mc, 1 - mc]

    def chunk(ch, _):
        for jj in range(NC):
            j = ch * NC + jj

            def block(i, _):
                at = pl.multiple_of(i * 16, 16)
                rows = pl.ds(at, 16)
                base, wave_add, seed_add = ints[0, rows], ints[1, rows], seed2[rows]
                a = amp[j, rows]
                for part in range(2):
                    f = a * noise(base, par[j, part], par[j, 2 + part], wave_add, seed_add)
                    hi, lo = split(f)
                    to = pl.ds(jj * N + at, 16)
                    xhi[to, part * DEPTH : (part + 1) * DEPTH] = hi
                    xlo[to, part * DEPTH : (part + 1) * DEPTH] = lo
                return 0

            lax.fori_loop(0, N // 16, block, 0, unroll=2)
        dot = lambda a, b: jnp.dot(a, b, preferred_element_type=F32)
        ybuf[...] = dot(xhi[...], inner[0]) + dot(xlo[...], inner[0]) + dot(xhi[...], inner[1])
        for jj in range(NC):
            yr, yi = ybuf[jj * N : (jj + 1) * N, :DEPTH], ybuf[jj * N : (jj + 1) * N, DEPTH:]
            tc, ts = twist[0], twist[1]
            hi, lo = split(jnp.concatenate([yr * tc - yi * ts, yr * ts + yi * tc], axis=0))
            z = dot(outer[0], hi) + dot(outer[0], lo) + dot(outer[1], hi)
            q = (ch * NC + jj) * 2
            zbuf[q] = z[:PAIRS]
            zbuf[q + 1] = z[PAIRS:]
        qs = pl.ds(ch * (2 * NC), 2 * NC)
        for t, (a, b, c, d) in enumerate(NEAR):
            if (a, b, c, d) == (0, 0, 0, 0):
                pltpu.make_async_copy(zbuf.at[qs, t], out.at[qs, pair], rsem.at[ch]).start()
            else:
                pltpu.make_async_remote_copy(
                    src_ref=zbuf.at[qs, t],
                    dst_ref=out.at[qs, pair],
                    send_sem=ssem.at[ch],
                    recv_sem=rsem.at[ch],
                    device_id=(xs[a] + zs[b] + ys[c] + cs[d],),
                    device_id_type=MESH,
                ).start()
        return 0

    lax.fori_loop(0, CHUNKS, chunk, 0)

    pltpu.make_async_copy(seeds_out, seeds_out, gsem).wait()
    for ch in range(CHUNKS):
        qs = pl.ds(ch * 2 * NC, 2 * NC)
        pltpu.make_async_copy(out.at[qs], out.at[qs], rsem.at[ch]).wait()
        sent = amp.at[pl.ds(0, 9), pl.ds(0, (PAIRS - 1) * 2 * NC // 9)]
        pltpu.make_async_copy(sent, sent, ssem.at[ch]).wait()


def turn(block, real, imag):
    for c, to in ((0, real), (1, imag)):
        to[...] = jnp.concatenate([block[c], block[2 + c]], axis=0).T


def shards(seeds, offset):
    ints, wave_sq, twist, inner, masks = tables()
    anywhere = pl.BlockSpec(memory_space=pl.ANY)
    scalar = pl.BlockSpec(memory_space=pltpu.SMEM)
    dma = pltpu.SemaphoreType.DMA
    blocks = pl.pallas_call(
        synth,
        out_shape=jax.ShapeDtypeStruct((Q, PAIRS, DEPTH), F32),
        in_specs=[scalar, scalar] + [anywhere] * 5,
        out_specs=anywhere,
        scratch_shapes=[
            pltpu.VMEM((2, N, DEPTH), jnp.int32),
            pltpu.VMEM((N, DEPTH), jnp.int32),
            pltpu.VMEM((N, DEPTH), F32),
            pltpu.VMEM((2, N, DEPTH), F32),
            pltpu.VMEM((2, 2 * DEPTH, 2 * DEPTH), BF16),
            pltpu.VMEM((PAIRS, N), jnp.int32),
            pltpu.VMEM((COLS, N, DEPTH), F32),
            pltpu.VMEM((NC * N, 2 * DEPTH), BF16),
            pltpu.VMEM((NC * N, 2 * DEPTH), BF16),
            pltpu.VMEM((NC * N, 2 * DEPTH), F32),
            pltpu.VMEM((Q, PAIRS, DEPTH), F32),
            pltpu.VMEM((2, 2 * PAIRS, 2 * N), BF16),
            pltpu.VMEM((8, N), jnp.int32),
            pltpu.VMEM((N, N), jnp.int32),
            pltpu.VMEM((N - 1, 1, N), jnp.int32),
            pltpu.SMEM((COLS, 4), jnp.int32),
            pltpu.SMEM((COLS,), F32),
            dma((5,)),
            dma,
            dma,
            dma((CHUNKS,)),
            dma((CHUNKS,)),
        ],
        compiler_params=pltpu.CompilerParams(
            collective_id=0, has_side_effects=True, vmem_limit_bytes=48 * 2**20
        ),
    )(offset, seeds, ints, wave_sq, twist, inner, masks)
    out = pl.BlockSpec((DEPTH, N), lambda i: (0, i))
    return pl.pallas_call(
        turn,
        grid=(STRIP // N,),
        out_shape=[jax.ShapeDtypeStruct((DEPTH, STRIP), F32)] * 2,
        in_specs=[pl.BlockSpec((4, PAIRS, DEPTH), lambda i: (i, 0, 0))],
        out_specs=[out, out],
    )(blocks)


def solution(mesh):
    in_specs = (P("rows"), P())
    out_specs = (P("rows", None), P("rows", None))
    return jax.shard_map(shards, mesh=mesh, in_specs=in_specs, out_specs=out_specs, check_vma=False)
```

time: 175 us -> 54.5 us (0.31)
  blocking collectives: 103 us -> 0 us
  Pallas kernels: 0 us -> 45.9 us
  waiting for transfers between devices: 30.1 us -> 0 us
  other arithmetic: 12.7 us -> 0 us
  local copies, waits for them, and re-layouts: 15 us -> 6.78 us
  matrix products: 6.79 us -> 0 us
  starting transfers between devices: 4.76 us -> 0 us
    unnamed x1 -> x0, blocking collectives: 68.7 us -> none
    pallas_call x0 -> x2, Pallas kernels: none -> 45.9 us  [the longest x1 40 us: shards(): pl.pallas_call(synth, out_shape=jax.ShapeDtypeStruct((Q, PAIRS, DEPTH), F...]
    all_to_all x1 -> x0, blocking collectives: 34.6 us -> none  [shards(): lax.all_to_all(combined, 'rows', split_axis=1, concat_axis=1, tiled=True)]
    all_to_all x1 -> x0, waiting for transfers between devices: 30.1 us -> none  [shards(): lax.all_to_all(turned, 'rows', split_axis=1, concat_axis=1, tiled=True)]
    mul x4 -> x0, other arithmetic: 9.33 us -> none  [the longest x1 8.19 us: spectrum(): return (amplitude * noise_real, amplitude * noise_imag)]
    dot_general x2 -> x0, matrix products: 6.79 us -> none  [the longest x1 3.58 us: shards(): jnp.dot(inner, stacked, preferred_element_type=jnp.float32, precision=lax...]
    reshape x3 -> x0, local copies, waits for them, and re-layouts: 5.29 us -> none  [the longest x2 3.35 us: shards(): combined = mixed.reshape(2, parts * share, count)]
    all_to_all x1 -> x0, starting transfers between devices: 4.76 us -> none  [shards(): lax.all_to_all(turned, 'rows', split_axis=1, concat_axis=1, tiled=True)]
  transfers between devices with their start and end apart: 1 -> 0, of which waited for: 1 -> 0; matrix products, arithmetic and copies ran while one was open for 0% -> 0% of each run, Pallas kernels for 0% -> 0%
where the time goes in v1:
time: 54.5 us; the launch traced here: 54 us
  Pallas kernels  45.9 us (84%)
  local copies, waits for them, and re-layouts  6.78 us (12%)
  between operations  1.31 us (2%)
    pallas_call x1, Pallas kernels, shards(): pl.pallas_call(synth, out_shape=jax.ShapeDtypeStruct((Q, PAIRS, DEPTH), F...  40 us
    unnamed x14, local copies, waits for them, and re-layouts  6.78 us
    pallas_call x1, Pallas kernels, shards(): pl.pallas_call(turn, grid=(STRIP // N,), out_shape=[jax.ShapeDtypeStruct(...  5.93 us

profile of v1, /device:TPU:1, one launch (start us, length us, event | category | flops | bytes accessed | tf_op | source)
XLA Modules:
  0.0 54.0 jit_solution(5490283710573562833)
XLA Ops:
  1.3 0.0 copy-start.1
  1.3 1.2 %copy-done.1 = bf16[2,512,512]{2,1,0:T(8,128)(2,1)S(1)} copy-done((bf16[2,512,512]{2,1,0:T(8,128)(2,1)S(1)}, bf16[2,512,512]{2,1,0:T(8,128)(2,1)}, u32[]{:S(2)}) %copy-start.1) | copy-done | bytes 1048600
  2.5 0.0 copy-start.2
  2.5 0.9 %copy-done.2 = f32[2,128,256]{2,1,0:T(8,128)S(1)} copy-done((f32[2,128,256]{2,1,0:T(8,128)S(1)}, f32[2,128,256]{2,1,0:T(8,128)}, u32[]{:S(2)}) %copy-start.2) | copy-done | bytes 262168
  3.5 0.0 copy-start.3
  3.5 0.9 %copy-done.3 = s32[2,128,256]{2,1,0:T(8,128)S(1)} copy-done((s32[2,128,256]{2,1,0:T(8,128)S(1)}, s32[2,128,256]{2,1,0:T(8,128)}, u32[]{:S(2)}) %copy-start.3) | copy-done | bytes 262168
  4.4 0.0 copy-start.4
  4.4 0.9 %copy-done.4 = f32[128,256]{1,0:T(8,128)S(1)} copy-done((f32[128,256]{1,0:T(8,128)S(1)}, f32[128,256]{1,0:T(8,128)}, u32[]{:S(2)}) %copy-start.4) | copy-done | bytes 131096
  5.3 0.0 copy-start.5
  5.3 0.8 %copy-done.5 = s32[64,128]{1,0:T(8,128)S(1)} copy-done((s32[64,128]{1,0:T(8,128)S(1)}, s32[64,128]{1,0:T(8,128)}, u32[]{:S(2)}) %copy-start.5) | copy-done | bytes 32792
  6.1 0.0 copy-start.6
  6.1 0.7 %copy-done.6 = s32[4]{0:T(128)S(1)} copy-done((s32[4]{0:T(128)S(1)}, s32[4]{0:T(128)}, u32[]{:S(2)}) %copy-start.6) | copy-done | bytes 40
  6.7 40.0 %shard_map.86.block = f32[32,64,256]{2,1,0:T(8,128)S(1)} custom-call(s32[1]{0:T(128)S(6)} %copy.9.offset, s32[4]{0:T(128)S(1)} %copy-done.6, s32[2,128,256]{2,1,0:T(8,128)S(1)} %copy-done.3, f32[128,256]{1,0:T(8,128)S(1)} %copy-done.4, f32[2,128,256]{2,1,0:T(8,128)S(1)} %copy-done.2, bf16[2,512,512]{2,1,0:T(8,128)(2,1)S(1)} %copy-done.1, s32[64,128]{1,0:T(8,128)S(1)} %copy-done.5), custom_call_target="tpu_custom_call" | custom-call | tf_op jit(solution)/shard_map/pallas_call | solution.py:286
  46.8 0.0 copy-start
  46.8 1.3 %copy-done = f32[32,64,256]{2,1,0:T(8,128)} copy-done((f32[32,64,256]{2,1,0:T(8,128)}, f32[32,64,256]{2,1,0:T(8,128)S(1)}, u32[]{:S(2)}) %copy-start) | copy-done | bytes 2097176
  48.1 5.9 %shard_map.87 = (f32[256,1024]{1,0:T(8,128)}, f32[256,1024]{1,0:T(8,128)}) custom-call(f32[32,64,256]{2,1,0:T(8,128)} %copy-done), custom_call_target="tpu_custom_call" | custom-call | tf_op jit(solution)/shard_map/pallas_call | solution.py:320
Async XLA Ops:
  1.3 1.2 %copy-start.1 = (bf16[2,512,512]{2,1,0:T(8,128)(2,1)S(1)}, bf16[2,512,512]{2,1,0:T(8,128)(2,1)}, u32[]{:S(2)}) copy-start(bf16[2,512,512]{2,1,0:T(8,128)(2,1)} %constant.13.clone.inner_hbm) | copy-start | bytes 3145732
  2.5 0.9 %copy-start.2 = (f32[2,128,256]{2,1,0:T(8,128)S(1)}, f32[2,128,256]{2,1,0:T(8,128)}, u32[]{:S(2)}) copy-start(f32[2,128,256]{2,1,0:T(8,128)} %constant.12.clone.twist_hbm) | copy-start | bytes 786436
  3.5 0.9 %copy-start.3 = (s32[2,128,256]{2,1,0:T(8,128)S(1)}, s32[2,128,256]{2,1,0:T(8,128)}, u32[]{:S(2)}) copy-start(s32[2,128,256]{2,1,0:T(8,128)} %constant.10.clone.ints_hbm) | copy-start | bytes 786436
  4.4 0.9 %copy-start.4 = (f32[128,256]{1,0:T(8,128)S(1)}, f32[128,256]{1,0:T(8,128)}, u32[]{:S(2)}) copy-start(f32[128,256]{1,0:T(8,128)} %constant.11.clone.wave_sq_hbm) | copy-start | bytes 393220
  5.3 0.8 %copy-start.5 = (s32[64,128]{1,0:T(8,128)S(1)}, s32[64,128]{1,0:T(8,128)}, u32[]{:S(2)}) copy-start(s32[64,128]{1,0:T(8,128)} %constant.14.clone.masks_hbm) | copy-start | bytes 98308
  6.1 0.7 %copy-start.6 = (s32[4]{0:T(128)S(1)}, s32[4]{0:T(128)}, u32[]{:S(2)}) copy-start(s32[4]{0:T(128)} %seeds.1) | copy-start | bytes 52
  46.8 1.4 %copy-start = (f32[32,64,256]{2,1,0:T(8,128)}, f32[32,64,256]{2,1,0:T(8,128)S(1)}, u32[]{:S(2)}) copy-start(f32[32,64,256]{2,1,0:T(8,128)S(1)} %shard_map.86.block) | copy-start | bytes 6291460

commit v2 on v1

v2 whole, which is shorter than its diff:
```python
import itertools
import math
import random

import jax
import jax.numpy as jnp
import numpy as np
from jax import lax
from jax.experimental import pallas as pl
from jax.experimental.pallas import tpu as pltpu
from jax.sharding import PartitionSpec as P

NY = 32768
NXG = 65536
STRIP = 1024
KAPPA = 8192
N = 128
DEPTH = 256
PAIRS = 64
COLS = STRIP // PAIRS
NC = 4
CHUNKS = COLS // NC
Q = 2 * COLS
MOD = 65521
MESH = pl.DeviceIdType.MESH
F32 = jnp.float32
BF16 = jnp.bfloat16


def hops(offset):
    return sum((0, 1, 2, 1)[a] for a in offset[:3])


def is_near(offset):
    if hops(offset) != 3:
        return hops(offset) < 3
    if 2 not in offset[:3]:
        return sum(a == 3 for a in offset[:3]) % 2 == 0
    return (offset.index(0) + 1) % 3 == offset[:3].index(2)


def near_offsets():
    every = itertools.product(range(4), range(4), range(4), range(2))
    near = [offset for offset in every if is_near(offset)]
    random.Random(3).shuffle(near)
    return near


NEAR = near_offsets()


MASKS = [((a * 4 + b) * 4 + c) * 2 + d for a, b, c, d in NEAR]


def split(x):
    hi = x.astype(BF16)
    return hi, (x - hi.astype(F32)).astype(BF16)


def mod_small(s, m):
    q = (s.astype(F32) * np.float32(1.0 / m)).astype(jnp.int32)
    r = s - q * m
    r = jnp.where(r < 0, r + m, r)
    return jnp.where(r >= m, r - m, r)


def noise(base, c1, c2, wave_add, seed_add):
    inv = np.float32(1.0 / MOD)
    t = base + c1
    t = jnp.where(t >= MOD, t - MOD, t)
    u = jnp.where(t >= 46337, t - 46337, t)
    p = u * u
    w = (p >> 16) * 32138 - (p & 0xFFFF) * 32802 + (wave_add + c2)
    w = w - (w >> 16) * MOD
    f = w.astype(F32)
    h = f - jnp.floor(f * inv + np.float32(0.5) * inv) * np.float32(MOD)
    u = jnp.where(h >= 46337.0, h - 46337.0, h).astype(jnp.int32)
    p = u * u + seed_add
    v = p - (p >> 16) * MOD
    x = v.astype(F32) * inv + np.float32(0.5 / MOD - 0.5)
    return x - jnp.round(x)


def xor_values(a):
    return [a, a + 1 - 2 * (a % 2), (a + 2) % 4, 3 - a]


def iota(shape, axis):
    return lax.broadcasted_iota(jnp.int32, shape, axis)


def cos_sin(m):
    n = (m + 4096) >> 13
    x = (m - (n << 13)).astype(F32) * np.float32(2.0 * math.pi / 32768)
    y = x * x
    s = x + x * y * (-1.0 / 6 + y * (1.0 / 120 + y * (-1.0 / 5040 + y * np.float32(1.0 / 362880))))
    c = 1.0 + y * (-0.5 + y * (1.0 / 24 + y * (-1.0 / 720 + y * np.float32(1.0 / 40320))))
    n = n & 3
    swap = (n & 1) == 1
    cos, sin = jnp.where(swap, s, c), jnp.where(swap, c, s)
    cos = jnp.where((n == 1) | (n == 2), -cos, cos)
    return cos, jnp.where(n >= 2, -sin, sin)


def wave_tables(i, base, wave_add, wave_sq, twist):
    rows = pl.ds(pl.multiple_of(i * 16, 16), 16)
    k1, k2 = iota((16, DEPTH), 0) + i * 16, iota((16, DEPTH), 1)
    k = k1 + N * k2
    h = k * 7919
    h = h - (h >> 16) * MOD
    base[rows] = jnp.where(h >= MOD, h - MOD, h)
    h = k - (k >> 13) * 8191
    h = jnp.where(h >= 8191, h - 8191, h)
    wave_add[rows] = h * 13 + 16000 * MOD
    ky = jnp.minimum(k, NY - k).astype(F32) * np.float32(1.0 / KAPPA)
    wave_sq[rows] = ky * ky + 1.0
    twist[0, rows], twist[1, rows] = cos_sin(k1 * k2)


def inner_rows(i, inner):
    at = pl.multiple_of(i * 16, 16)
    c, s = cos_sin(((iota((16, DEPTH), 0) + at) * iota((16, DEPTH), 1) & (DEPTH - 1)) * (NY // DEPTH))
    for x, down, right in ((c, 0, 0), (s, 0, 1), (-s, 1, 0), (c, 1, 1)):
        hi, lo = split(x)
        rows, cols = pl.ds(DEPTH * down + at, 16), pl.ds(DEPTH * right, DEPTH)
        inner[0, rows, cols] = hi
        inner[1, rows, cols] = lo


def synth(
    offset, seeds, out,
    base, wave_add, wave_sq, seed_add, twist, inner, outer, amp, xhi, xlo, ybuf, zbuf,
    seed_row, seed_all, par, parf, rows_out, sent, gsend, grecv, ssem, rsem,
):
    me = lax.axis_index("rows")
    mx, mz, my, mc = me // 32, me // 8 % 4, me // 2 % 4, me % 2
    mxz, myc = me // 8, me % 8
    barrier = pltpu.get_barrier_semaphore()
    across = [(mxz + i) % 16 * 8 + myc for i in range(1, 16)]
    along = [mxz * 8 + (myc + i) % 8 for i in range(1, 8)]
    for peer in across + along:
        pl.semaphore_signal(barrier, inc=1, device_id=(peer,), device_id_type=MESH)

    lane = iota((8, N), 1)
    odd, half = lane % 2, lane // 2 % 2
    seed_row[...] = jnp.where(
        half == 0, jnp.where(odd == 0, seeds[0], seeds[2]), jnp.where(odd == 0, seeds[1], seeds[3])
    )

    upper = mx // 2
    flip = lambda a: (a + 2 * upper) % 4
    pair = (mx % 2) * 32 + flip(mz) * 8 + flip(my) * 2 + mc

    def prepare(i, _):
        wave_tables(i, base, wave_add, wave_sq, twist)
        return 0

    def exchange_seeds():
        pl.semaphore_wait(barrier, 22)
        pltpu.make_async_copy(seed_row.at[0], seed_all.at[myc, mxz], grecv.at[0]).start()
        for peer in across:
            pltpu.make_async_remote_copy(
                src_ref=seed_row.at[0],
                dst_ref=seed_all.at[myc, mxz],
                send_sem=gsend.at[0],
                recv_sem=grecv.at[0],
                device_id=(peer,),
                device_id_type=MESH,
            ).start()

    def forward_seeds():
        pltpu.make_async_copy(seed_all.at[0], seed_all.at[0], grecv.at[0]).wait()
        for peer in along:
            pltpu.make_async_remote_copy(
                src_ref=seed_all.at[myc],
                dst_ref=seed_all.at[myc],
                send_sem=gsend.at[1],
                recv_sem=grecv.at[1],
                device_id=(peer,),
                device_id_type=MESH,
            ).start()

    lax.fori_loop(0, N // 16, prepare, 0)
    exchange_seeds()

    for j in range(COLS):
        g = offset[0] + (j * PAIRS + pair)
        c = g * 30011 % MOD
        d = g % 4099 * 7
        par[j, 0] = (c + 17) % MOD
        par[j, 1] = (c + 29011) % MOD
        par[j, 2] = (d + 17) * 32719 % MOD
        par[j, 3] = (d + 29011) * 32719 % MOD
        kx = jnp.minimum(g, NXG - g).astype(F32) * np.float32(1.0 / KAPPA)
        parf[j] = kx * kx

    for at in range(0, PAIRS, 8):
        dest = jnp.concatenate([jnp.full((1, N), m, jnp.int32) for m in MASKS[at : at + 8]], axis=0)
        dest = lax.bitwise_xor(dest, me)
        c, s = cos_sin((dest * iota((8, N), 1) & (N - 1)) * (NY // N))
        for x, i, k in ((c, 0, 0), (-s, 0, 1), (s, 1, 0), (c, 1, 1)):
            ybuf[pl.ds(PAIRS * i + at, 8), pl.ds(N * k, N)] = x
    hi, lo = split(ybuf[: 2 * PAIRS, : 2 * N])
    outer[0] = hi
    outer[1] = lo

    def prepare_inner(i, _):
        inner_rows(i, inner)
        return 0

    forward_seeds()
    lax.fori_loop(0, DEPTH // 16, prepare_inner, 0)

    scale = np.float32(2.0 * 3.4641016151377544 / math.sqrt(NY))

    def amplitude(i, _):
        rows = pl.ds(pl.multiple_of(i * 16, 16), 16)
        z0 = wave_sq[rows]
        for j in range(COLS):
            y = lax.rsqrt(z0 + parf[j])
            amp[j, rows] = y * y * lax.rsqrt(y) * scale
        return 0

    lax.fori_loop(0, N // 16, amplitude, 0)

    pltpu.make_async_copy(seed_all.at[pl.ds(0, 7)], seed_all.at[pl.ds(0, 7)], grecv.at[1]).wait()

    got = seed_all[...].reshape(N, N)
    turned = pltpu.roll(got, 2, 1)
    lane, row = iota((N, N), 1), iota((N, N), 0)
    owner = row % 16 * 8 + row // 16
    for h in range(2):
        picked = jnp.where(lane // 2 % 2 == h, got, turned)
        for t in range(2):
            s = jnp.where(lane // 2 + 64 * t == owner, picked, 0).astype(F32)
            s = jnp.sum(s, axis=0, keepdims=True).astype(jnp.int32)
            rows, cols = pl.ds(64 * h, 64), pl.ds(128 * t, 128)
            a = base[rows, cols] + jnp.broadcast_to(mod_small(s, MOD), (64, 128))
            base[rows, cols] = jnp.where(a >= MOD, a - MOD, a)
            seed_add[rows, cols] = jnp.broadcast_to(mod_small(s, 32749), (64, 128))

    xs, zs = [v * 32 for v in xor_values(mx)], [v * 8 for v in xor_values(mz)]
    ys, cs = [v * 2 for v in xor_values(my)], [mc, 1 - mc]
    dot = lambda a, b: jnp.dot(a, b, preferred_element_type=F32)

    def chunk(ch, _):
        for jj in range(NC):
            j = ch * NC + jj

            def block(i, _):
                at = pl.multiple_of(i * 16, 16)
                rows = pl.ds(at, 16)
                b, w, s, a = base[rows], wave_add[rows], seed_add[rows], amp[j, rows]
                for part in range(2):
                    hi, lo = split(a * noise(b, par[j, part], par[j, 2 + part], w, s))
                    to = pl.ds(jj * N + at, 16)
                    xhi[to, part * DEPTH : (part + 1) * DEPTH] = hi
                    xlo[to, part * DEPTH : (part + 1) * DEPTH] = lo
                return 0

            lax.fori_loop(0, N // 16, block, 0, unroll=2)
        ybuf[...] = dot(xhi[...], inner[0]) + dot(xlo[...], inner[0]) + dot(xhi[...], inner[1])
        for jj in range(NC):
            yr, yi = ybuf[jj * N : (jj + 1) * N, :DEPTH], ybuf[jj * N : (jj + 1) * N, DEPTH:]
            tc, ts = twist[0], twist[1]
            hi, lo = split(jnp.concatenate([yr * tc - yi * ts, yr * ts + yi * tc], axis=0))
            z = dot(outer[0], hi) + dot(outer[0], lo) + dot(outer[1], hi)
            q = (ch * NC + jj) * 2
            zbuf[q] = z[:PAIRS]
            zbuf[q + 1] = z[PAIRS:]
        qs = pl.ds(ch * (2 * NC), 2 * NC)
        for t, (a, b, c, d) in enumerate(NEAR):
            if (a, b, c, d) == (0, 0, 0, 0):
                pltpu.make_async_copy(zbuf.at[qs, t], out.at[qs, pair], rsem.at[ch]).start()
            else:
                pltpu.make_async_remote_copy(
                    src_ref=zbuf.at[qs, t],
                    dst_ref=out.at[qs, pair],
                    send_sem=ssem.at[ch],
                    recv_sem=rsem.at[ch],
                    device_id=(xs[a] + zs[b] + ys[c] + cs[d],),
                    device_id_type=MESH,
                ).start()
        return 0

    lax.fori_loop(0, CHUNKS, chunk, 0)

    pltpu.make_async_copy(rows_out, rows_out, gsend.at[0]).wait()
    pltpu.make_async_copy(seed_all.at[pl.ds(0, 7)], seed_all.at[pl.ds(0, 7)], gsend.at[1]).wait()
    for ch in range(CHUNKS):
        qs = pl.ds(ch * 2 * NC, 2 * NC)
        pltpu.make_async_copy(out.at[qs], out.at[qs], rsem.at[ch]).wait()
        pltpu.make_async_copy(sent, sent, ssem.at[ch]).wait()


def turn(blocks, real, imag, turned, sems):
    eye = (iota((DEPTH, DEPTH), 0) == iota((DEPTH, DEPTH), 1)).astype(F32).astype(BF16)
    dot = lambda x: lax.dot_general(eye, x, (((1,), (1,)), ((), ())), preferred_element_type=F32)
    copies = []
    for i in range(STRIP // 256):
        for part, to in ((0, real), (1, imag)):
            rows = jnp.concatenate([blocks[8 * i + 2 * j + part] for j in range(4)], axis=0)
            hi, lo = split(rows)
            cols = pl.ds(256 * i, 256)
            turned[part, :, cols] = dot(hi) + dot(lo)
            copies.append(pltpu.make_async_copy(turned.at[part, :, cols], to.at[:, cols], sems.at[i, part]))
            copies[-1].start()
    for copy in copies:
        copy.wait()


def shards(seeds, offset):
    scalar = pl.BlockSpec(memory_space=pltpu.SMEM)
    hbm = pl.BlockSpec(memory_space=pltpu.HBM)
    dma = pltpu.SemaphoreType.DMA
    vmem = pltpu.VMEM
    blocks = pl.pallas_call(
        synth,
        out_shape=jax.ShapeDtypeStruct((Q, PAIRS, DEPTH), F32),
        in_specs=[scalar, scalar],
        out_specs=pl.BlockSpec(memory_space=pl.ANY),
        scratch_shapes=[
            vmem((N, DEPTH), jnp.int32),
            vmem((N, DEPTH), jnp.int32),
            vmem((N, DEPTH), F32),
            vmem((N, DEPTH), jnp.int32),
            vmem((2, N, DEPTH), F32),
            vmem((2, 2 * DEPTH, 2 * DEPTH), BF16),
            vmem((2, 2 * PAIRS, 2 * N), BF16),
            vmem((COLS, N, DEPTH), F32),
            vmem((NC * N, 2 * DEPTH), BF16),
            vmem((NC * N, 2 * DEPTH), BF16),
            vmem((NC * N, 2 * DEPTH), F32),
            vmem((Q, PAIRS, DEPTH), F32),
            vmem((8, N), jnp.int32),
            vmem((8, 16, N), jnp.int32),
            pltpu.SMEM((COLS, 4), jnp.int32),
            pltpu.SMEM((COLS,), F32),
            vmem((15, 1, N), jnp.int32),
            vmem((PAIRS - 1, 2 * NC, 1, DEPTH), F32),
            dma((2,)),
            dma((2,)),
            dma((CHUNKS,)),
            dma((CHUNKS,)),
        ],
        compiler_params=pltpu.CompilerParams(
            collective_id=0, has_side_effects=True, vmem_limit_bytes=48 * 2**20
        ),
    )(offset, seeds)
    return pl.pallas_call(
        turn,
        out_shape=[jax.ShapeDtypeStruct((DEPTH, STRIP), F32)] * 2,
        in_specs=[pl.BlockSpec(memory_space=pltpu.VMEM)],
        out_specs=[hbm, hbm],
        scratch_shapes=[vmem((2, DEPTH, STRIP), F32), dma((STRIP // 256, 2))],
        compiler_params=pltpu.CompilerParams(vmem_limit_bytes=16 * 2**20),
    )(blocks)


def solution(mesh):
    in_specs = (P("rows"), P())
    out_specs = (P("rows", None), P("rows", None))
    return jax.shard_map(shards, mesh=mesh, in_specs=in_specs, out_specs=out_specs, check_vma=False)
```

time: 54.5 us -> 43.8 us (0.80)
  local copies, waits for them, and re-layouts: 6.78 us -> 0.65 us
  Pallas kernels: 45.9 us -> 41.7 us
    unnamed x14 -> x2, local copies, waits for them, and re-layouts: 6.78 us -> 0.65 us
    pallas_call x1, Pallas kernels: 5.93 us -> 1.71 us  [shards(): pl.pallas_call(turn, out_shape=[jax.ShapeDtypeStruct((DEPTH, STRIP), F32)...]
where the time goes in v2:
time: 43.8 us; the launch traced here: 43.7 us
  Pallas kernels  41.7 us (95%)
  between operations  1.29 us (3%)
  local copies, waits for them, and re-layouts  0.65 us (1%)
    pallas_call x1, Pallas kernels, shards(): pl.pallas_call(synth, out_shape=jax.ShapeDtypeStruct((Q, PAIRS, DEPTH), F...  40 us
    pallas_call x1, Pallas kernels, shards(): pl.pallas_call(turn, out_shape=[jax.ShapeDtypeStruct((DEPTH, STRIP), F32)...  1.71 us

profile of v2, /device:TPU:1, one launch (start us, length us, event | category | flops | bytes accessed | tf_op | source)
XLA Modules:
  0.0 43.7 jit_solution(2913339792783454867)
XLA Ops:
  1.3 0.0 copy-start
  1.3 0.6 %copy-done = s32[4]{0:T(128)S(1)} copy-done((s32[4]{0:T(128)S(1)}, s32[4]{0:T(128)}, u32[]{:S(2)}) %copy-start) | copy-done | bytes 40
  1.9 40.0 %shard_map.41.blocks = f32[32,64,256]{2,1,0:T(8,128)S(1)} custom-call(s32[1]{0:T(128)S(6)} %copy.4.offset, s32[4]{0:T(128)S(1)} %copy-done), custom_call_target="tpu_custom_call" | custom-call | tf_op jit(solution)/shard_map/pallas_call | solution.py:317
  42.0 1.7 %shard_map.42 = (f32[256,1024]{1,0:T(8,128)}, f32[256,1024]{1,0:T(8,128)}) custom-call(f32[32,64,256]{2,1,0:T(8,128)S(1)} %shard_map.41.blocks), custom_call_target="tpu_custom_call" | custom-call | tf_op jit(solution)/shard_map/pallas_call | solution.py:350
Async XLA Ops:
  1.3 0.7 %copy-start = (s32[4]{0:T(128)S(1)}, s32[4]{0:T(128)}, u32[]{:S(2)}) copy-start(s32[4]{0:T(128)} %seeds.1) | copy-start | bytes 52

commit v3 on v2

v3 whole, which is shorter than its diff:
```python
import itertools
import math
import random

import jax
import jax.numpy as jnp
import numpy as np
from jax import lax
from jax.experimental import pallas as pl
from jax.experimental.pallas import tpu as pltpu
from jax.sharding import PartitionSpec as P

NY = 32768
NXG = 65536
STRIP = 1024
KAPPA = 8192
N = 128
DEPTH = 256
PAIRS = 64
COLS = STRIP // PAIRS
SIZES = (2, 2, 3, 4, 5)
STARTS = tuple(sum(SIZES[:i]) for i in range(len(SIZES)))
NC = max(SIZES)
Q = 2 * COLS
MOD = 65521
MESH = pl.DeviceIdType.MESH
F32 = jnp.float32
BF16 = jnp.bfloat16


def hops(offset):
    return sum((0, 1, 2, 1)[a] for a in offset[:3])


def is_near(offset):
    if hops(offset) != 3:
        return hops(offset) < 3
    if 2 not in offset[:3]:
        return sum(a == 3 for a in offset[:3]) % 2 == 0
    return (offset.index(0) + 1) % 3 == offset[:3].index(2)


def near_offsets():
    every = itertools.product(range(4), range(4), range(4), range(2))
    near = [offset for offset in every if is_near(offset)]
    random.Random(3).shuffle(near)
    near.sort(key=hops, reverse=True)
    return near


NEAR = near_offsets()


OTHERS = list(itertools.product(range(4), range(4), range(4), range(2)))[1:]
FAR_FIRST = sorted(OTHERS, key=hops, reverse=True)
MASKS = [((a * 4 + b) * 4 + c) * 2 + d for a, b, c, d in NEAR]


def split(x):
    hi = x.astype(BF16)
    return hi, (x - hi.astype(F32)).astype(BF16)


def mod_small(s, m):
    q = (s.astype(F32) * np.float32(1.0 / m)).astype(jnp.int32)
    r = s - q * m
    r = jnp.where(r < 0, r + m, r)
    return jnp.where(r >= m, r - m, r)


def noise(base, c, wave_add, seed_add):
    low, high, add0, add1, add2, mix = c
    u = base + jnp.where(base < high, jnp.where(base < low, add0, add1), add2)
    p = u * u
    w = p * 32719 + (p >> 15) * (16069 - 32719 * 32768) + (wave_add + mix)
    w = w - (w >> 16) * MOD
    w = w - (w >> 16) * MOD
    u = w - jnp.where(w < 46337, 0, jnp.where(w < MOD, 46337, MOD))
    p = u * u
    return (p * 65551 + (p >> 16) * 225 + seed_add).astype(F32)


def xor_values(a):
    return [a, a + 1 - 2 * (a % 2), (a + 2) % 4, 3 - a]


def iota(shape, axis):
    return lax.broadcasted_iota(jnp.int32, shape, axis)


def cos_sin(m):
    n = (m + 4096) >> 13
    x = (m - (n << 13)).astype(F32) * np.float32(2.0 * math.pi / 32768)
    y = x * x
    s = x + x * y * (-1.0 / 6 + y * (1.0 / 120 + y * (-1.0 / 5040 + y * np.float32(1.0 / 362880))))
    c = 1.0 + y * (-0.5 + y * (1.0 / 24 + y * (-1.0 / 720 + y * np.float32(1.0 / 40320))))
    n = n & 3
    swap = (n & 1) == 1
    cos, sin = jnp.where(swap, s, c), jnp.where(swap, c, s)
    cos = jnp.where((n == 1) | (n == 2), -cos, cos)
    return cos, jnp.where(n >= 2, -sin, sin)


def lane_row(lane):
    return (lane & (N - 1)) * 2 + (lane >> 7)


def wave_tables(i, base, wave_add, wave_sq, twist):
    rows = pl.ds(pl.multiple_of(i * 16, 16), 16)
    k1, k2 = iota((16, DEPTH), 0) + i * 16, iota((16, DEPTH), 1)
    k = k1 + N * k2
    h = k * 7919
    h = h - (h >> 16) * MOD
    base[rows] = jnp.where(h >= MOD, h - MOD, h)
    h = k - (k >> 13) * 8191
    h = jnp.where(h >= 8191, h - 8191, h)
    wave_add[rows] = h * 13
    ky = jnp.minimum(k, NY - k).astype(F32) * np.float32(1.0 / KAPPA)
    wave_sq[rows] = ky * ky + 1.0
    twist[0, rows], twist[1, rows] = cos_sin(k1 * lane_row(k2))


def inner_rows(i, inner):
    at = pl.multiple_of(i * 16, 16)
    row = lane_row(iota((16, DEPTH), 1))
    c, s = cos_sin(((iota((16, DEPTH), 0) + at) * row & (DEPTH - 1)) * (NY // DEPTH))
    for x, down, right in ((c, 0, 0), (s, 0, 1), (-s, 1, 0), (c, 1, 1)):
        hi, lo = split(x)
        cols = pl.ds(N * right, N)
        for part, y in enumerate((hi, hi, lo)):
            rows = pl.ds(DEPTH * part + N * down + at, 16)
            inner[0, rows, cols] = y[:, :N]
            inner[1, rows, cols] = y[:, N:]


def synth(
    offset, seeds_hbm, out,
    base, wave_add, wave_sq, seed_add, twist, inner, outer, amp, xhi, xlo, ybuf, zbuf,
    seed_row, seed_all, par, parf, rows_out, sent, seeds, seeds_sem, gsend, grecv, ssem, rsem,
):
    me = lax.axis_index("rows")
    mx, mz, my, mc = me // 32, me // 8 % 4, me // 2 % 4, me % 2
    xs, zs = [v * 32 for v in xor_values(mx)], [v * 8 for v in xor_values(mz)]
    ys, cs = [v * 2 for v in xor_values(my)], [mc, 1 - mc]
    device = lambda offset: (xs[offset[0]] + zs[offset[1]] + ys[offset[2]] + cs[offset[3]],)
    own = pltpu.make_async_copy(seeds_hbm, seeds, seeds_sem)
    own.start()
    barrier = pltpu.get_barrier_semaphore()
    for to in FAR_FIRST:
        pl.semaphore_signal(barrier, inc=1, device_id=device(to), device_id_type=MESH)

    own.wait()
    lane = iota((8, N), 1)
    odd, half = lane % 2, lane // 2 % 2
    seed_row[...] = jnp.where(
        half == 0, jnp.where(odd == 0, seeds[0], seeds[2]), jnp.where(odd == 0, seeds[1], seeds[3])
    )

    upper = mx // 2
    flip = lambda a: (a + 2 * upper) % 4
    pair = (mx % 2) * 32 + flip(mz) * 8 + flip(my) * 2 + mc

    def prepare(i, _):
        wave_tables(i, base, wave_add, wave_sq, twist)
        return 0

    pl.semaphore_wait(barrier, N - 1)
    pltpu.make_async_copy(seed_row.at[0], seed_all.at[me], grecv).start()
    for to in FAR_FIRST:
        pltpu.make_async_remote_copy(
            src_ref=seed_row.at[0],
            dst_ref=seed_all.at[me],
            send_sem=gsend,
            recv_sem=grecv,
            device_id=device(to),
            device_id_type=MESH,
        ).start()

    lax.fori_loop(0, N // 16, prepare, 0)

    for j in range(COLS):
        g = offset[0] + (j * PAIRS + pair)
        hashed, mixed = g * 30011 % MOD, g % 4099 * 7
        for part, salt in enumerate((17, 29011)):
            c = (hashed + salt) % MOD
            below = c < 46337
            low, high = jnp.where(below, 46337 - c, MOD - c), jnp.where(below, MOD - c, MOD + 46337 - c)
            add0 = jnp.where(below, c, c - 46337)
            add1 = jnp.where(below, c - 46337, c - MOD)
            add2 = jnp.where(below, c - MOD, c - MOD - 46337)
            for i, x in enumerate((low, high, add0, add1, add2, (mixed + salt) * 32719 % MOD)):
                par[j, 6 * part + i] = x
        kx = jnp.minimum(g, NXG - g).astype(F32) * np.float32(1.0 / KAPPA)
        parf[j] = kx * kx

    for at in range(0, PAIRS, 8):
        dest = jnp.concatenate([jnp.full((1, N), m, jnp.int32) for m in MASKS[at : at + 8]], axis=0)
        dest = lax.bitwise_xor(dest, me)
        c, s = cos_sin((dest * iota((8, N), 1) & (N - 1)) * (NY // N))
        for x, i, k in ((c, 0, 0), (-s, 0, 1), (s, 1, 0), (c, 1, 1)):
            ybuf[pl.ds(PAIRS * i + at, 8), pl.ds(N * k, N)] = x
    hi, lo = split(ybuf[: 2 * PAIRS, : 2 * N])
    for part, x in enumerate((hi, hi, lo)):
        outer[:, 2 * N * part : 2 * N * (part + 1)] = x

    def prepare_inner(i, _):
        inner_rows(i, inner)
        return 0

    lax.fori_loop(0, N // 16, prepare_inner, 0)

    scale = np.float32(2.0 * 3.4641016151377544 / math.sqrt(NY) / 2.0**32)

    def amplitude(i, _):
        rows = pl.ds(pl.multiple_of(i * 16, 16), 16)
        z0 = wave_sq[rows]
        for j in range(COLS):
            y = lax.rsqrt(z0 + parf[j])
            amp[j, rows] = y * y * lax.rsqrt(y) * scale
        return 0

    lax.fori_loop(0, N // 16, amplitude, 0)

    pltpu.make_async_copy(seed_all, seed_all, grecv).wait()

    got = seed_all[...]
    turned = pltpu.roll(got, 2, 1)
    lane, row = iota((N, N), 1), iota((N, N), 0)
    for h in range(2):
        picked = jnp.where(lane // 2 % 2 == h, got, turned)
        for t in range(2):
            s = jnp.where(lane // 2 + 64 * t == row, picked, 0).astype(F32)
            s = jnp.sum(s, axis=0, keepdims=True).astype(jnp.int32)
            rows, cols = pl.ds(64 * h, 64), pl.ds(128 * t, 128)
            a = base[rows, cols] + jnp.broadcast_to(mod_small(s, MOD), (64, 128))
            base[rows, cols] = jnp.where(a >= MOD, a - MOD, a)
            seed_add[rows, cols] = jnp.broadcast_to(mod_small(s, 32749) * 65551 + (32776 + 128 - 2**31), (64, 128))

    dot = lambda a, b: jnp.dot(a, b, preferred_element_type=F32)

    def chunk(ch, start, size):
        for jj in range(size):
            j = start + jj

            def block(i, _):
                at = pl.multiple_of(i * 16, 16)
                rows = pl.ds(at, 16)
                b, w, s, a = base[rows], wave_add[rows], seed_add[rows], amp[j, rows]
                into = pl.ds(jj * N + at, 16)
                for part in range(2):
                    f = a * noise(b, [par[j, 6 * part + i] for i in range(6)], w, s)
                    even, odd = f[:, :N] + f[:, N:], f[:, :N] - f[:, N:]
                    for parity, x in enumerate((even, odd)):
                        cols = pl.ds(DEPTH * parity + N * part, N)
                        xhi[into, cols], xlo[into, cols] = split(x)
                return 0

            lax.fori_loop(0, N // 16, block, 0, unroll=8)
        for parity in range(2):
            cols = pl.ds(DEPTH * parity, DEPTH)
            high, low = xhi[: size * N, cols], xlo[: size * N, cols]
            ybuf[: size * N, cols] = dot(jnp.concatenate([high, low, high], axis=1), inner[parity])
        for jj in range(size):
            rows = pl.ds(jj * N, N)
            yr = jnp.concatenate([ybuf[rows, 0 * N : 1 * N], ybuf[rows, 2 * N : 3 * N]], axis=1)
            yi = jnp.concatenate([ybuf[rows, 1 * N : 2 * N], ybuf[rows, 3 * N : 4 * N]], axis=1)
            tc, ts = twist[0], twist[1]
            hi, lo = split(jnp.concatenate([yr * tc - yi * ts, yr * ts + yi * tc], axis=0))
            z = dot(outer[...], jnp.concatenate([hi, lo, hi], axis=0))
            q = (start + jj) * 2
            zbuf[q] = z[:PAIRS]
            zbuf[q + 1] = z[PAIRS:]
        qs = pl.ds(2 * start, 2 * size)
        for t, to in enumerate(NEAR):
            if to == (0, 0, 0, 0):
                pltpu.make_async_copy(zbuf.at[qs, t], out.at[qs, pair], rsem.at[ch]).start()
            else:
                pltpu.make_async_remote_copy(
                    src_ref=zbuf.at[qs, t],
                    dst_ref=out.at[qs, pair],
                    send_sem=ssem.at[ch],
                    recv_sem=rsem.at[ch],
                    device_id=device(to),
                    device_id_type=MESH,
                ).start()

    for ch, (start, size) in enumerate(zip(STARTS, SIZES)):
        chunk(ch, start, size)

    pltpu.make_async_copy(rows_out, rows_out, gsend).wait()
    for ch, (start, size) in enumerate(zip(STARTS, SIZES)):
        qs = pl.ds(2 * start, 2 * size)
        pltpu.make_async_copy(out.at[qs], out.at[qs], rsem.at[ch]).wait()
        gone = sent.at[:, pl.ds(0, 2 * size)]
        pltpu.make_async_copy(gone, gone, ssem.at[ch]).wait()


def turn(blocks, real, imag, turned, sems):
    order = (iota((DEPTH, DEPTH), 0) == lane_row(iota((DEPTH, DEPTH), 1))).astype(F32).astype(BF16)
    dot = lambda x: lax.dot_general(order, x, (((1,), (1,)), ((), ())), preferred_element_type=F32)
    copies = []
    for i in range(STRIP // 256):
        for part, to in ((0, real), (1, imag)):
            rows = jnp.concatenate([blocks[8 * i + 2 * j + part] for j in range(4)], axis=0)
            hi, lo = split(rows)
            cols = pl.ds(256 * i, 256)
            turned[part, :, cols] = dot(hi) + dot(lo)
            copies.append(pltpu.make_async_copy(turned.at[part, :, cols], to.at[:, cols], sems.at[i, part]))
            copies[-1].start()
    for copy in copies:
        copy.wait()


def shards(seeds, offset):
    scalar = pl.BlockSpec(memory_space=pltpu.SMEM)
    hbm = pl.BlockSpec(memory_space=pltpu.HBM)
    dma = pltpu.SemaphoreType.DMA
    vmem = pltpu.VMEM
    blocks = pl.pallas_call(
        synth,
        out_shape=jax.ShapeDtypeStruct((Q, PAIRS, DEPTH), F32),
        in_specs=[scalar, hbm],
        out_specs=pl.BlockSpec(memory_space=pl.ANY),
        scratch_shapes=[
            vmem((N, DEPTH), jnp.int32),
            vmem((N, DEPTH), jnp.int32),
            vmem((N, DEPTH), F32),
            vmem((N, DEPTH), jnp.int32),
            vmem((2, N, DEPTH), F32),
            vmem((2, 3 * DEPTH, DEPTH), BF16),
            vmem((2 * PAIRS, 3 * 2 * N), BF16),
            vmem((COLS, N, DEPTH), F32),
            vmem((NC * N, 2 * DEPTH), BF16),
            vmem((NC * N, 2 * DEPTH), BF16),
            vmem((NC * N, 2 * DEPTH), F32),
            vmem((Q, PAIRS, DEPTH), F32),
            vmem((8, N), jnp.int32),
            vmem((N, N), jnp.int32),
            pltpu.SMEM((COLS, 12), jnp.int32),
            pltpu.SMEM((COLS,), F32),
            vmem((N - 1, 1, N), jnp.int32),
            vmem((PAIRS - 1, 2 * NC, 1, DEPTH), F32),
            pltpu.SMEM((4,), jnp.int32),
            dma,
            dma,
            dma,
            dma((len(SIZES),)),
            dma((len(SIZES),)),
        ],
        compiler_params=pltpu.CompilerParams(
            collective_id=0, has_side_effects=True, vmem_limit_bytes=48 * 2**20
        ),
    )(offset, seeds)
    return pl.pallas_call(
        turn,
        out_shape=[jax.ShapeDtypeStruct((DEPTH, STRIP), F32)] * 2,
        in_specs=[pl.BlockSpec(memory_space=pltpu.VMEM)],
        out_specs=[hbm, hbm],
        scratch_shapes=[vmem((2, DEPTH, STRIP), F32), dma((STRIP // 256, 2))],
        compiler_params=pltpu.CompilerParams(vmem_limit_bytes=16 * 2**20),
    )(blocks)


def solution(mesh):
    in_specs = (P("rows"), P())
    out_specs = (P("rows", None), P("rows", None))
    return jax.shard_map(shards, mesh=mesh, in_specs=in_specs, out_specs=out_specs, check_vma=False)
```

time: 43.8 us -> 38.9 us (0.89)
  Pallas kernels: 41.7 us -> 36.9 us
    pallas_call x1, Pallas kernels: 40 us -> 35.1 us  [shards(): pl.pallas_call(synth, out_shape=jax.ShapeDtypeStruct((Q, PAIRS, DEPTH), F...]
where the time goes in v3:
time: 38.9 us; the launch traced here: 38.8 us
  Pallas kernels  36.9 us (95%)
  between operations  1.29 us (3%)
  local copies, waits for them, and re-layouts  0.65 us (2%)
    pallas_call x1, Pallas kernels, shards(): pl.pallas_call(synth, out_shape=jax.ShapeDtypeStruct((Q, PAIRS, DEPTH), F...  35.1 us
    pallas_call x1, Pallas kernels, shards(): pl.pallas_call(turn, out_shape=[jax.ShapeDtypeStruct((DEPTH, STRIP), F32)...  1.72 us

profile of v3, /device:TPU:1, one launch (start us, length us, event | category | flops | bytes accessed | tf_op | source)
XLA Modules:
  0.0 38.8 jit_solution(4705396193242039700)
XLA Ops:
  1.3 0.0 copy-start
  1.3 0.6 %copy-done = s32[4]{0:T(128)S(1)} copy-done((s32[4]{0:T(128)S(1)}, s32[4]{0:T(128)}, u32[]{:S(2)}) %copy-start) | copy-done | bytes 40
  1.9 35.1 %shard_map.41.blocks = f32[32,64,256]{2,1,0:T(8,128)S(1)} custom-call(s32[1]{0:T(128)S(6)} %copy.4.offset, s32[4]{0:T(128)S(1)} %copy-done), custom_call_target="tpu_custom_call" | custom-call | tf_op jit(solution)/shard_map/pallas_call | solution.py:319
  37.1 1.7 %shard_map.42 = (f32[256,1024]{1,0:T(8,128)}, f32[256,1024]{1,0:T(8,128)}) custom-call(f32[32,64,256]{2,1,0:T(8,128)S(1)} %shard_map.41.blocks), custom_call_target="tpu_custom_call" | custom-call | tf_op jit(solution)/shard_map/pallas_call | solution.py:354
Async XLA Ops:
  1.3 0.7 %copy-start = (s32[4]{0:T(128)S(1)}, s32[4]{0:T(128)}, u32[]{:S(2)}) copy-start(s32[4]{0:T(128)} %seeds_hbm.1) | copy-start | bytes 52

commit v4 on v3

--- a/solution.py
+++ b/solution.py
@@ -17,11 +17,12 @@
 N = 128
 DEPTH = 256
 PAIRS = 64
-COLS = STRIP // PAIRS
-SIZES = (2, 2, 3, 4, 5)
-STARTS = tuple(sum(SIZES[:i]) for i in range(len(SIZES)))
-NC = max(SIZES)
-Q = 2 * COLS
+QUADS = 32
+CHUNKS = ((0, 0, 2), (0, 2, 2), (0, 4, 3), (0, 7, 5), (1, 0, 4), (1, 4, 4))
+PAIR_COLS = sum(size for kind, _, size in CHUNKS if kind == 0)
+QUAD_COLS = sum(size for kind, _, size in CHUNKS if kind == 1)
+COLS = PAIR_COLS + QUAD_COLS
+NC = max(size for _, _, size in CHUNKS)
 MOD = 65521
 MESH = pl.DeviceIdType.MESH
 F32 = jnp.float32
@@ -53,7 +54,16 @@
 
 OTHERS = list(itertools.product(range(4), range(4), range(4), range(2)))[1:]
 FAR_FIRST = sorted(OTHERS, key=hops, reverse=True)
-MASKS = [((a * 4 + b) * 4 + c) * 2 + d for a, b, c, d in NEAR]
+NEAR_QUAD = [
+    (a, b ^ c, d, e)
+    for a, b in ((0, 0), (1, 0), (3, 0), (0, 1))
+    for c, d in ((0, 0), (3, 0), (0, 1), (0, 3))
+    for e in range(2)
+]
+random.Random(4).shuffle(NEAR_QUAD)
+NEAR_QUAD.sort(key=hops, reverse=True)
+SERVED = (NEAR, NEAR_QUAD)
+MASKS = [((a * 4 + b) * 4 + c) * 2 + d for served in SERVED for a, b, c, d in served]
 
 
 def split(x):
@@ -134,8 +144,8 @@
 
 
 def synth(
-    offset, seeds_hbm, out,
-    base, wave_add, wave_sq, seed_add, twist, inner, outer, amp, xhi, xlo, ybuf, zbuf,
+    offset, seeds_hbm, pair_out, quad_out,
+    base, wave_add, wave_sq, seed_add, twist, inner, pair_outer, quad_outer, amp, xhi, xlo, ybuf, pair_z, quad_z,
     seed_row, seed_all, par, parf, rows_out, sent, seeds, seeds_sem, gsend, grecv, ssem, rsem,
 ):
     me = lax.axis_index("rows")
@@ -160,6 +170,15 @@
     flip = lambda a: (a + 2 * upper) % 4
     pair = (mx % 2) * 32 + flip(mz) * 8 + flip(my) * 2 + mc
 
+    xg, zg, yg = mx // 2, mz // 2, my // 2
+    x0, z0, y0 = (mx + xg) % 2, (mz + zg) % 2, (my + yg) % 2
+    quad = (((x0 + xg) % 2 * 2 + (z0 + xg) % 2) * 2 + (zg + yg) % 2) * 2 + (y0 + yg) % 2
+    quad = quad * 2 + mc
+    kinds = (
+        (NEAR, pair, pair_outer, pair_z, pair_out),
+        (NEAR_QUAD, quad, quad_outer, quad_z, quad_out),
+    )
+
     def prepare(i, _):
         wave_tables(i, base, wave_add, wave_sq, twist)
         return 0
@@ -179,7 +198,10 @@
     lax.fori_loop(0, N // 16, prepare, 0)
 
     for j in range(COLS):
-        g = offset[0] + (j * PAIRS + pair)
+        if j < PAIR_COLS:
+            g = offset[0] + (j * PAIRS + pair)
+        else:
+            g = offset[0] + (PAIR_COLS * PAIRS + (j - PAIR_COLS) * QUADS + quad)
         hashed, mixed = g * 30011 % MOD, g % 4099 * 7
         for part, salt in enumerate((17, 29011)):
             c = (hashed + salt) % MOD
@@ -193,15 +215,17 @@
         kx = jnp.minimum(g, NXG - g).astype(F32) * np.float32(1.0 / KAPPA)
         parf[j] = kx * kx
 
-    for at in range(0, PAIRS, 8):
+    for at in range(0, PAIRS + QUADS, 8):
         dest = jnp.concatenate([jnp.full((1, N), m, jnp.int32) for m in MASKS[at : at + 8]], axis=0)
         dest = lax.bitwise_xor(dest, me)
         c, s = cos_sin((dest * iota((8, N), 1) & (N - 1)) * (NY // N))
+        first, count = (0, PAIRS) if at < PAIRS else (PAIRS, QUADS)
         for x, i, k in ((c, 0, 0), (-s, 0, 1), (s, 1, 0), (c, 1, 1)):
-            ybuf[pl.ds(PAIRS * i + at, 8), pl.ds(N * k, N)] = x
-    hi, lo = split(ybuf[: 2 * PAIRS, : 2 * N])
-    for part, x in enumerate((hi, hi, lo)):
-        outer[:, 2 * N * part : 2 * N * (part + 1)] = x
+            ybuf[pl.ds(first + count * i + at, 8), pl.ds(N * k, N)] = x
+    for outer, first in ((pair_outer, 0), (quad_outer, 2 * PAIRS)):
+        hi, lo = split(ybuf[first : first + outer.shape[0], : 2 * N])
+        for part, x in enumerate((hi, hi, lo)):
+            outer[:, 2 * N * part : 2 * N * (part + 1)] = x
 
     def prepare_inner(i, _):
         inner_rows(i, inner)
@@ -238,9 +262,11 @@
 
     dot = lambda a, b: jnp.dot(a, b, preferred_element_type=F32)
 
-    def chunk(ch, start, size):
+    def chunk(ch, kind, start, size):
+        served, group, outer, zbuf, out = kinds[kind]
+        count = len(served)
         for jj in range(size):
-            j = start + jj
+            j = kind * PAIR_COLS + start + jj
 
             def block(i, _):
                 at = pl.multiple_of(i * 16, 16)
@@ -268,40 +294,45 @@
             hi, lo = split(jnp.concatenate([yr * tc - yi * ts, yr * ts + yi * tc], axis=0))
             z = dot(outer[...], jnp.concatenate([hi, lo, hi], axis=0))
             q = (start + jj) * 2
-            zbuf[q] = z[:PAIRS]
-            zbuf[q + 1] = z[PAIRS:]
+            zbuf[q] = z[:count]
+            zbuf[q + 1] = z[count:]
         qs = pl.ds(2 * start, 2 * size)
-        for t, to in enumerate(NEAR):
+        for t, to in enumerate(served):
             if to == (0, 0, 0, 0):
-                pltpu.make_async_copy(zbuf.at[qs, t], out.at[qs, pair], rsem.at[ch]).start()
+                pltpu.make_async_copy(zbuf.at[qs, t], out.at[qs, group], rsem.at[ch]).start()
             else:
                 pltpu.make_async_remote_copy(
                     src_ref=zbuf.at[qs, t],
-                    dst_ref=out.at[qs, pair],
+                    dst_ref=out.at[qs, group],
                     send_sem=ssem.at[ch],
                     recv_sem=rsem.at[ch],
                     device_id=device(to),
                     device_id_type=MESH,
                 ).start()
 
-    for ch, (start, size) in enumerate(zip(STARTS, SIZES)):
-        chunk(ch, start, size)
+    for ch, (kind, start, size) in enumerate(CHUNKS):
+        chunk(ch, kind, start, size)
 
     pltpu.make_async_copy(rows_out, rows_out, gsend).wait()
-    for ch, (start, size) in enumerate(zip(STARTS, SIZES)):
+    for ch, (kind, start, size) in enumerate(CHUNKS):
+        served, out = kinds[kind][0], kinds[kind][-1]
         qs = pl.ds(2 * start, 2 * size)
         pltpu.make_async_copy(out.at[qs], out.at[qs], rsem.at[ch]).wait()
-        gone = sent.at[:, pl.ds(0, 2 * size)]
+        gone = sent.at[pl.ds(0, len(served) - 1), pl.ds(0, 2 * size)]
         pltpu.make_async_copy(gone, gone, ssem.at[ch]).wait()
 
 
-def turn(blocks, real, imag, turned, sems):
+def turn(pairs, quads, real, imag, turned, sems):
     order = (iota((DEPTH, DEPTH), 0) == lane_row(iota((DEPTH, DEPTH), 1))).astype(F32).astype(BF16)
     dot = lambda x: lax.dot_general(order, x, (((1,), (1,)), ((), ())), preferred_element_type=F32)
     copies = []
     for i in range(STRIP // 256):
         for part, to in ((0, real), (1, imag)):
-            rows = jnp.concatenate([blocks[8 * i + 2 * j + part] for j in range(4)], axis=0)
+            if i < PAIR_COLS // 4:
+                rows = [pairs[8 * i + 2 * j + part] for j in range(4)]
+            else:
+                rows = [quads[16 * (i - PAIR_COLS // 4) + 2 * j + part] for j in range(8)]
+            rows = jnp.concatenate(rows, axis=0)
             hi, lo = split(rows)
             cols = pl.ds(256 * i, 256)
             turned[part, :, cols] = dot(hi) + dot(lo)
@@ -316,11 +347,14 @@
     hbm = pl.BlockSpec(memory_space=pltpu.HBM)
     dma = pltpu.SemaphoreType.DMA
     vmem = pltpu.VMEM
-    blocks = pl.pallas_call(
+    pairs, quads = pl.pallas_call(
         synth,
-        out_shape=jax.ShapeDtypeStruct((Q, PAIRS, DEPTH), F32),
+        out_shape=[
+            jax.ShapeDtypeStruct((2 * PAIR_COLS, PAIRS, DEPTH), F32),
+            jax.ShapeDtypeStruct((2 * QUAD_COLS, QUADS, DEPTH), F32),
+        ],
         in_specs=[scalar, hbm],
-        out_specs=pl.BlockSpec(memory_space=pl.ANY),
+        out_specs=[pl.BlockSpec(memory_space=pl.ANY)] * 2,
         scratch_shapes=[
             vmem((N, DEPTH), jnp.int32),
             vmem((N, DEPTH), jnp.int32),
@@ -329,11 +363,13 @@
             vmem((2, N, DEPTH), F32),
             vmem((2, 3 * DEPTH, DEPTH), BF16),
             vmem((2 * PAIRS, 3 * 2 * N), BF16),
+            vmem((2 * QUADS, 3 * 2 * N), BF16),
             vmem((COLS, N, DEPTH), F32),
             vmem((NC * N, 2 * DEPTH), BF16),
             vmem((NC * N, 2 * DEPTH), BF16),
             vmem((NC * N, 2 * DEPTH), F32),
-            vmem((Q, PAIRS, DEPTH), F32),
+            vmem((2 * PAIR_COLS, PAIRS, DEPTH), F32),
+            vmem((2 * QUAD_COLS, QUADS, DEPTH), F32),
             vmem((8, N), jnp.int32),
             vmem((N, N), jnp.int32),
             pltpu.SMEM((COLS, 12), jnp.int32),
@@ -344,8 +380,8 @@
             dma,
             dma,
             dma,
-            dma((len(SIZES),)),
-            dma((len(SIZES),)),
+            dma((len(CHUNKS),)),
+            dma((len(CHUNKS),)),
         ],
         compiler_params=pltpu.CompilerParams(
             collective_id=0, has_side_effects=True, vmem_limit_bytes=48 * 2**20
@@ -354,11 +390,11 @@
     return pl.pallas_call(
         turn,
         out_shape=[jax.ShapeDtypeStruct((DEPTH, STRIP), F32)] * 2,
-        in_specs=[pl.BlockSpec(memory_space=pltpu.VMEM)],
+        in_specs=[pl.BlockSpec(memory_space=pltpu.VMEM)] * 2,
         out_specs=[hbm, hbm],
         scratch_shapes=[vmem((2, DEPTH, STRIP), F32), dma((STRIP // 256, 2))],
         compiler_params=pltpu.CompilerParams(vmem_limit_bytes=16 * 2**20),
-    )(blocks)
+    )(pairs, quads)
 
 
 def solution(mesh):

time: 38.9 us -> 38.4 us (0.987)
  Pallas kernels: 36.9 us -> 36.2 us
    pallas_call x1, Pallas kernels: 35.1 us -> 34.5 us  [shards(): pl.pallas_call(synth, out_shape=[jax.ShapeDtypeStruct((2 * PAIR_COLS, PAI...]
where the time goes in v4:
time: 38.4 us; the launch traced here: 38.3 us
  Pallas kernels  36.2 us (94%)
  between operations  1.45 us (4%)
  local copies, waits for them, and re-layouts  0.65 us (2%)
    pallas_call x1, Pallas kernels, shards(): pl.pallas_call(synth, out_shape=[jax.ShapeDtypeStruct((2 * PAIR_COLS, PAI...  34.5 us
    pallas_call x1, Pallas kernels, shards(): pl.pallas_call(turn, out_shape=[jax.ShapeDtypeStruct((DEPTH, STRIP), F32)...  1.72 us

profile of v4, /device:TPU:1, one launch (start us, length us, event | category | flops | bytes accessed | tf_op | source)
XLA Modules:
  0.0 38.3 jit_solution(11342220559612207391)
XLA Ops:
  1.3 0.0 copy-start
  1.3 0.6 %copy-done = s32[4]{0:T(128)S(1)} copy-done((s32[4]{0:T(128)S(1)}, s32[4]{0:T(128)}, u32[]{:S(2)}) %copy-start) | copy-done | bytes 40
  1.9 34.5 %shard_map.41 = (f32[24,64,256]{2,1,0:T(8,128)S(1)}, f32[16,32,256]{2,1,0:T(8,128)S(1)}) custom-call(s32[1]{0:T(128)S(6)} %copy.4.offset, s32[4]{0:T(128)S(1)} %copy-done), custom_call_target="tpu_custom_call" | custom-call | tf_op jit(solution)/shard_map/pallas_call | solution.py:350
  36.4 1.7 %shard_map.42 = (f32[256,1024]{1,0:T(8,128)}, f32[256,1024]{1,0:T(8,128)}) custom-call(f32[24,64,256]{2,1,0:T(8,128)S(1)} %get-tuple-element.4.pairs, f32[16,32,256]{2,1,0:T(8,128)S(1)} %get-tuple-element.5.quads), custom_call_target="tpu_custom_call" | custom-call | tf_op jit(solution)/shard_map/pallas_call | solution.py:390
Async XLA Ops:
  1.3 0.7 %copy-start = (s32[4]{0:T(128)S(1)}, s32[4]{0:T(128)}, u32[]{:S(2)}) copy-start(s32[4]{0:T(128)} %seeds_hbm.1) | copy-start | bytes 52

commit v5 on v4

--- a/solution.py
+++ b/solution.py
@@ -350,8 +350,8 @@
     pairs, quads = pl.pallas_call(
         synth,
         out_shape=[
-            jax.ShapeDtypeStruct((2 * PAIR_COLS, PAIRS, DEPTH), F32),
-            jax.ShapeDtypeStruct((2 * QUAD_COLS, QUADS, DEPTH), F32),
+            vmem((2 * PAIR_COLS, PAIRS, DEPTH), F32),
+            vmem((2 * QUAD_COLS, QUADS, DEPTH), F32),
         ],
         in_specs=[scalar, hbm],
         out_specs=[pl.BlockSpec(memory_space=pl.ANY)] * 2,
@@ -384,7 +384,7 @@
             dma((len(CHUNKS),)),
         ],
         compiler_params=pltpu.CompilerParams(
-            collective_id=0, has_side_effects=True, vmem_limit_bytes=48 * 2**20
+            collective_id=0, has_side_effects=True, vmem_limit_bytes=52 * 2**20
         ),
     )(offset, seeds)
     return pl.pallas_call(

time: 38.4 us -> 38 us (0.990)
  local copies, waits for them, and re-layouts: 0.65 us -> 0 us
    unnamed x2 -> x0, local copies, waits for them, and re-layouts: 0.65 us -> none
where the time goes in v5:
time: 38 us; the launch traced here: 37.9 us
  Pallas kernels  36.4 us (96%)
  between operations  1.44 us (4%)
    pallas_call x1, Pallas kernels, shards(): pl.pallas_call(synth, out_shape=[vmem((2 * PAIR_COLS, PAIRS, DEPTH), F32)...  34.7 us
    pallas_call x1, Pallas kernels, shards(): pl.pallas_call(turn, out_shape=[jax.ShapeDtypeStruct((DEPTH, STRIP), F32)...  1.71 us

profile of v5, /device:TPU:1, one launch (start us, length us, event | category | flops | bytes accessed | tf_op | source)
XLA Modules:
  0.0 37.9 jit_solution(8454548854897204877)
XLA Ops:
  1.3 34.7 %shard_map.41 = (f32[24,64,256]{2,1,0:T(8,128)S(1)}, f32[16,32,256]{2,1,0:T(8,128)S(1)}) custom-call(s32[1]{0:T(128)S(6)} %copy.4.offset, s32[4]{0:T(128)} %seeds_hbm.1), custom_call_target="tpu_custom_call" | custom-call | tf_op jit(solution)/shard_map/pallas_call | solution.py:350
  36.0 1.7 %shard_map.42 = (f32[256,1024]{1,0:T(8,128)}, f32[256,1024]{1,0:T(8,128)}) custom-call(f32[24,64,256]{2,1,0:T(8,128)S(1)} %get-tuple-element.4.pairs, f32[16,32,256]{2,1,0:T(8,128)S(1)} %get-tuple-element.5.quads), custom_call_target="tpu_custom_call" | custom-call | tf_op jit(solution)/shard_map/pallas_call | solution.py:390
